TPU v7x, 1024 devices: a whole 8x8x8 slice. The times are simulated.
1024 devices in a mesh: gy: 16 (over x, y_hi), gz: 64 (over z, y_lo, core).
Axes of the slice: x: 8, y: 8 (y_hi: 2, y_lo: 4; y = y_hi * 4 + y_lo), z: 8, core: 2. Of those that a mesh axis runs over, the one named last changes fastest.
Arguments:
- fields: float32 [8, 512, 128, 256], P(None, 'gz', 'gy'), may hold values from -5 to 5
- accum: float32 [8, 512, 128, 256], P(None, 'gz', 'gy'), may hold values from -4 to 4
Outputs:
- new_fields: float32 [8, 512, 128, 256], P(None, 'gz', 'gy')
- new_accum: float32 [8, 512, 128, 256], P(None, 'gz', 'gy')
- time_step: float32 [1], replicated
All inputs are finite; a program needn't handle non-finite values.
Results may differ from a plain program's by a relative error of at most 0.0003.
Values sent between devices are 32-bit elements; how exact they have to be, the bound alone decides.
A program may use at most 32 MiB of HBM per device.

v0:
```python
import jax
import jax.numpy as jnp
from jax import lax
from jax.sharding import PartitionSpec as P


def extended(cells, sides, width):
    for axis, dim in sides:
        count = lax.axis_size(axis)
        head = lax.slice_in_dim(cells, 0, width, axis=dim)
        tail = lax.slice_in_dim(cells, cells.shape[dim] - width, cells.shape[dim], axis=dim)
        cells = jnp.concatenate(
            [
                lax.ppermute(tail, axis, [(i, (i + 1) % count) for i in range(count)]),
                cells,
                lax.ppermute(head, axis, [((i + 1) % count, i) for i in range(count)]),
            ],
            axis=dim,
        )
    return cells


def shifted(block, dim, step):
    count = block.shape[dim] - 6
    return lax.slice_in_dim(block, 3 + step, 3 + step + count, axis=dim)


def first_pad(block, dim):
    return (
        45.0 * (shifted(block, dim, 1) - shifted(block, dim, -1))
        - 9.0 * (shifted(block, dim, 2) - shifted(block, dim, -2))
        + (shifted(block, dim, 3) - shifted(block, dim, -3))
    ) / 60.0


def second_pad(block, dim):
    return (
        -490.0 * shifted(block, dim, 0)
        + 270.0 * (shifted(block, dim, 1) + shifted(block, dim, -1))
        - 27.0 * (shifted(block, dim, 2) + shifted(block, dim, -2))
        + 2.0 * (shifted(block, dim, 3) + shifted(block, dim, -3))
    ) / 180.0


def rolled(block, step):
    return jnp.roll(block, -step, axis=3)


def first_x(block):
    return (
        45.0 * (rolled(block, 1) - rolled(block, -1))
        - 9.0 * (rolled(block, 2) - rolled(block, -2))
        + (rolled(block, 3) - rolled(block, -3))
    ) / 60.0


def second_x(block):
    return (
        -490.0 * block
        + 270.0 * (rolled(block, 1) + rolled(block, -1))
        - 27.0 * (rolled(block, 2) + rolled(block, -2))
        + 2.0 * (rolled(block, 3) + rolled(block, -3))
    ) / 180.0


def tendency(padded):
    inner = padded[:, 3:-3, 3:-3]
    grad = (first_x(inner), first_pad(padded[:, 3:-3], 2), first_pad(padded[:, :, 3:-3], 1))
    diag = (second_x(inner), second_pad(padded[:, 3:-3], 2), second_pad(padded[:, :, 3:-3], 1))
    mixed_xy = first_x(grad[1])
    mixed_xz = first_x(grad[2])
    mixed_yz = first_pad(first_pad(padded, 1), 2)
    table = ((None, mixed_xy, mixed_xz), (mixed_xy, None, mixed_yz), (mixed_xz, mixed_yz, None))

    def hess(i, j, k):
        if i == j:
            return diag[i][k]
        return table[i][j][k]

    def lap(k):
        return diag[0][k] + diag[1][k] + diag[2][k]

    lnrho = inner[0]
    ss = inner[4]
    vel = [inner[1], inner[2], inner[3]]

    def dvel(i, j):
        return grad[j][1 + i]

    def dpot(i, j):
        return grad[j][5 + i]

    field_b = [dpot(2, 1) - dpot(1, 2), dpot(0, 2) - dpot(2, 0), dpot(1, 0) - dpot(0, 1)]
    current = [hess(i, 0, 5) + hess(i, 1, 6) + hess(i, 2, 7) - lap(5 + i) for i in range(3)]
    divu = dvel(0, 0) + dvel(1, 1) + dvel(2, 2)
    strain = [
        [0.5 * (dvel(i, j) + dvel(j, i)) - (divu / 3.0 if i == j else 0.0) for j in range(3)]
        for i in range(3)
    ]
    reciprocal_mass_per_volume = jnp.exp(-lnrho)
    acoustic_wave_celerity = jnp.exp(5.0 / 3.0 * ss + 2.0 / 3.0 * lnrho)
    thermal_level = 1.5 * acoustic_wave_celerity

    def transport_flux(k):
        return vel[0] * grad[0][k] + vel[1] * grad[1][k] + vel[2] * grad[2][k]

    lorentz = [
        current[1] * field_b[2] - current[2] * field_b[1],
        current[2] * field_b[0] - current[0] * field_b[2],
        current[0] * field_b[1] - current[1] * field_b[0],
    ]
    uxb = [
        vel[1] * field_b[2] - vel[2] * field_b[1],
        vel[2] * field_b[0] - vel[0] * field_b[2],
        vel[0] * field_b[1] - vel[1] * field_b[0],
    ]
    total_change_rate = [-transport_flux(0) - divu]
    for i in range(3):
        viscous = (
            lap(1 + i)
            + (hess(i, 0, 1) + hess(i, 1, 2) + hess(i, 2, 3)) / 3.0
            + 2.0
            * (strain[i][0] * grad[0][0] + strain[i][1] * grad[1][0] + strain[i][2] * grad[2][0])
        )
        total_change_rate.append(
            -transport_flux(1 + i)
            - acoustic_wave_celerity * (grad[i][4] + grad[i][0])
            + lorentz[i] * reciprocal_mass_per_volume
            + 0.1 * viscous
        )
    deformation_norm = sum((strain[i][j] * strain[i][j] for i in range(3) for j in range(3)))
    electric_flow_norm = current[0] * current[0] + current[1] * current[1] + current[2] * current[2]
    total_change_rate.append(
        -transport_flux(4)
        + (2.0 * 0.1 * deformation_norm + 0.1 * electric_flow_norm * reciprocal_mass_per_volume)
        / thermal_level
    )
    for i in range(3):
        total_change_rate.append(uxb[i] + 0.1 * lap(5 + i))
    b_sq = field_b[0] * field_b[0] + field_b[1] * field_b[1] + field_b[2] * field_b[2]
    rate = (
        jnp.abs(vel[0])
        + jnp.abs(vel[1])
        + jnp.abs(vel[2])
        + jnp.sqrt(acoustic_wave_celerity + b_sq * reciprocal_mass_per_volume)
    )
    return (jnp.max(rate), jnp.stack(total_change_rate))


def local(fields, accum):
    padded = extended(fields, (("gy", 2), ("gz", 1)), 3)
    local_rate, rhs = tendency(padded)
    fastest = lax.pmax(local_rate, ("gy", "gz"))
    time_step = 0.4 / fastest
    new_accum = -5.0 / 9.0 * accum + rhs
    new_fields = fields + 15.0 / 16.0 * time_step * new_accum
    return (new_fields, new_accum, jnp.reshape(time_step, (1,)))


def solution(mesh):
    in_specs = (P(None, "gz", "gy", None), P(None, "gz", "gy", None))
    out_specs = (P(None, "gz", "gy", None), P(None, "gz", "gy", None), P())
    return jax.shard_map(local, mesh=mesh, in_specs=in_specs, out_specs=out_specs, check_vma=False)
```

profile of v0, /device:TPU:1, one launch (start us, length us, event | category | flops | bytes accessed | tf_op | source)
XLA Modules:
  0.0 209.0 jit_solution(8961260074053508421)
XLA Ops:
  0.6 1.4 fusion.68
  2.0 8.7 %collective-permute-start.1 = (f32[8,8,3,256]{3,2,1,0:T(4,128)S(1)}, f32[8,8,3,256]{3,2,1,0:T(4,128)S(1)}, u32[]{:S(2)}, u32[]{:S(2)}) collective-permute-start(f32[8,8,3,256]{3,2,1,0:T(4,128)S(1)} %get-tuple-element.63), channel_id=1, source_target_pairs={{0,64},{64,128},{128,192},{192,256},{256,320},{320,384},{384,448},... | collective-permute-start | bytes 589832 | tf_op jit(solution)/shard_map/ppermute | solution.py:14
  10.8 4.2 %collective-permute-start = (f32[8,8,3,256]{3,2,1,0:T(4,128)S(1)}, f32[8,8,3,256]{3,2,1,0:T(4,128)S(1)}, u32[]{:S(2)}, u32[]{:S(2)}) collective-permute-start(f32[8,8,3,256]{3,2,1,0:T(4,128)S(1)} %get-tuple-element.64), channel_id=1, source_target_pairs={{64,0},{128,64},{192,128},{256,192},{320,256},{384,320},{448,384},... | collective-permute-start | bytes 589832 | tf_op jit(solution)/shard_map/ppermute | solution.py:16
  15.0 1.2 fusion.67
  17.1 1.5 add_multiply_fusion.1
  19.3 6.3 %collective-permute-done = f32[8,8,3,256]{3,2,1,0:T(4,128)S(1)} collective-permute-done((f32[8,8,3,256]{3,2,1,0:T(4,128)S(1)}, f32[8,8,3,256]{3,2,1,0:T(4,128)S(1)}, u32[]{:S(2)}, u32[]{:S(2)}) %collective-permute-start) | collective-permute-done | bytes 196640 | tf_op jit(solution)/shard_map/ppermute | solution.py:16
  25.6 3.2 %collective-permute-done.1 = f32[8,8,3,256]{3,2,1,0:T(4,128)S(1)} collective-permute-done((f32[8,8,3,256]{3,2,1,0:T(4,128)S(1)}, f32[8,8,3,256]{3,2,1,0:T(4,128)S(1)}, u32[]{:S(2)}, u32[]{:S(2)}) %collective-permute-start.1) | collective-permute-done | bytes 196640 | tf_op jit(solution)/shard_map/ppermute | solution.py:14
  28.8 1.5 add_multiply_fusion.2
  31.2 0.9 fusion.50
  32.1 1.1 fusion.55
  33.2 1.1 fusion.51
  34.5 11.5 %collective-permute-start.2 = (f32[8,3,14,256]{3,2,1,0:T(8,128)S(1)}, f32[8,3,14,256]{3,2,1,0:T(8,128)S(1)}, u32[]{:S(2)}, u32[]{:S(2)}) collective-permute-start(f32[8,3,14,256]{3,2,1,0:T(8,128)S(1)} %get-tuple-element.23), channel_id=1, source_target_pairs={{1,0},{2,1},{3,2},{4,3},{5,4},{6,5},{7,6},{8,7},{9,8},{10,9},{11,1... | collective-permute-start | bytes 1032200 | tf_op jit(solution)/shard_map/ppermute | solution.py:16
  46.1 1.9 collective-permute-start.3
  48.0 0.9 fusion.54
  48.9 1.1 fusion.53
  50.1 16.8 %collective-permute-done.3 = f32[8,3,14,256]{3,2,1,0:T(8,128)S(1)} collective-permute-done((f32[8,3,14,256]{3,2,1,0:T(8,128)S(1)}, f32[8,3,14,256]{3,2,1,0:T(8,128)S(1)}, u32[]{:S(2)}, u32[]{:S(2)}) %collective-permute-start.3) | collective-permute-done | bytes 344096 | tf_op jit(solution)/shard_map/ppermute | solution.py:14
  67.7 1.3 add_multiply_fusion
  72.9 1.2 fusion.61
  74.1 1.1 fusion.57
  75.2 1.1 fusion.59
  76.3 118.5 %pmax.7 = f32[]{:T(128)} all-reduce(f32[]{:T(128)} %get-tuple-element.5), channel_id=1, replica_groups=mesh['gy'=16,'gz'=64] {'gy','gz'}, use_global_device_ids=true, to_apply=%region_1.2 | all-reduce | flops 1 | bytes 8 | tf_op jit(solution)/shard_map/pmax | solution.py:153
  194.9 3.1 %fusion.20 = f32[8,8,8,256]{3,2,1,0:T(8,128)S(1)} fusion(f32[8,8,8,1]{3,2,1,0:T(8,128)} %get-tuple-element.48, f32[8,8,8,255]{3,2,1,0:T(8,128)} %get-tuple-element.50, f32[8,8,8,255]{3,2,1,0:T(8,128)} %get-tuple-element.49, f32[8,8,8,1]{3,2,1,0:T(8,128)} %get-tuple-element.47, f32[8,8,8,2]{3,2,1,0:T(8,128)} %get-tuple-element.44, ...), kind=kLoop, calls=%fused_computation.43 | loop fusion | flops 1835008 | bytes 3670016 | tf_op jit(solution)/shard_map/div | solution.py:50
  198.6 0.9 fusion.8
  205.7 2.1 %multiply_add_fusion = (f32[8,8,8,256]{3,2,1,0:T(8,128)}, f32[8,8,8,256]{3,2,1,0:T(8,128)}) fusion(f32[8,8,8,256]{3,2,1,0:T(8,128)S(1)} %copy-done, f32[]{:T(128)S(6)} %mul_shard_map.3, f32[8,8,8,256]{3,2,1,0:T(8,128)} %add_dynamic-update-slice_fusion, f32[8,8,8,256]{3,2,1,0:T(8,128)S(1)} %copy-done.16), kind=kLoop, calls=%fused_computation.47 | loop fusion | flops 524288 | bytes 2621444 | tf_op jit(solution)/shard_map/add | solution.py:156
  (58 shorter events, 13.5 us)
Async XLA Ops:
  0.6 15.5 %copy-start = (f32[8,8,8,256]{3,2,1,0:T(8,128)S(1)}, f32[8,8,8,256]{3,2,1,0:T(8,128)}, u32[]{:S(2)}) copy-start(f32[8,8,8,256]{3,2,1,0:T(8,128)} %param.2) | copy-start | bytes 1572868
  2.0 26.8 %collective-permute-start.1 = (f32[8,8,3,256]{3,2,1,0:T(4,128)S(1)}, f32[8,8,3,256]{3,2,1,0:T(4,128)S(1)}, u32[]{:S(2)}, u32[]{:S(2)}) collective-permute-start(f32[8,8,3,256]{3,2,1,0:T(4,128)S(1)} %get-tuple-element.63), channel_id=1, source_target_pairs={{0,64},{64,128},{128,192},{192,256},{256,320},{320,384},{384,448},... | collective-permute-start | bytes 589832 | tf_op jit(solution)/shard_map/ppermute | solution.py:14
  10.8 14.8 %collective-permute-start = (f32[8,8,3,256]{3,2,1,0:T(4,128)S(1)}, f32[8,8,3,256]{3,2,1,0:T(4,128)S(1)}, u32[]{:S(2)}, u32[]{:S(2)}) collective-permute-start(f32[8,8,3,256]{3,2,1,0:T(4,128)S(1)} %get-tuple-element.64), channel_id=1, source_target_pairs={{64,0},{128,64},{192,128},{256,192},{320,256},{384,320},{448,384},... | collective-permute-start | bytes 589832 | tf_op jit(solution)/shard_map/ppermute | solution.py:16
  34.5 15.6 %collective-permute-start.2 = (f32[8,3,14,256]{3,2,1,0:T(8,128)S(1)}, f32[8,3,14,256]{3,2,1,0:T(8,128)S(1)}, u32[]{:S(2)}, u32[]{:S(2)}) collective-permute-start(f32[8,3,14,256]{3,2,1,0:T(8,128)S(1)} %get-tuple-element.23), channel_id=1, source_target_pairs={{1,0},{2,1},{3,2},{4,3},{5,4},{6,5},{7,6},{8,7},{9,8},{10,9},{11,1... | collective-permute-start | bytes 1032200 | tf_op jit(solution)/shard_map/ppermute | solution.py:16
  46.1 20.9 %collective-permute-start.3 = (f32[8,3,14,256]{3,2,1,0:T(8,128)S(1)}, f32[8,3,14,256]{3,2,1,0:T(8,128)S(1)}, u32[]{:S(2)}, u32[]{:S(2)}) collective-permute-start(f32[8,3,14,256]{3,2,1,0:T(8,128)S(1)} %get-tuple-element.24), channel_id=1, source_target_pairs={{0,1},{1,2},{2,3},{3,4},{4,5},{5,6},{6,7},{7,8},{8,9},{9,10},{10,1... | collective-permute-start | bytes 1032200 | tf_op jit(solution)/shard_map/ppermute | solution.py:14
  194.8 3.2 %copy-start.4 = (f32[8,8,8,255]{3,2,1,0:T(8,128)S(1)}, f32[8,8,8,255]{3,2,1,0:T(8,128)}, u32[]{:S(2)}) copy-start(f32[8,8,8,255]{3,2,1,0:T(8,128)} %get-tuple-element.37) | copy-start | bytes 1566724
  194.8 3.2 %copy-start.5 = (f32[8,8,8,255]{3,2,1,0:T(8,128)S(1)}, f32[8,8,8,255]{3,2,1,0:T(8,128)}, u32[]{:S(2)}) copy-start(f32[8,8,8,255]{3,2,1,0:T(8,128)} %get-tuple-element.38) | copy-start | bytes 1566724
  194.8 3.2 %copy-start.6 = (f32[8,8,8,253]{3,2,1,0:T(8,128)S(1)}, f32[8,8,8,253]{3,2,1,0:T(8,128)}, u32[]{:S(2)}) copy-start(f32[8,8,8,253]{3,2,1,0:T(8,128)} %get-tuple-element.29) | copy-start | bytes 1554436
  194.8 3.2 %copy-start.7 = (f32[8,8,8,253]{3,2,1,0:T(8,128)S(1)}, f32[8,8,8,253]{3,2,1,0:T(8,128)}, u32[]{:S(2)}) copy-start(f32[8,8,8,253]{3,2,1,0:T(8,128)} %get-tuple-element.30) | copy-start | bytes 1554436
  194.8 3.2 %copy-start.8 = (f32[8,8,8,254]{3,2,1,0:T(8,128)S(1)}, f32[8,8,8,254]{3,2,1,0:T(8,128)}, u32[]{:S(2)}) copy-start(f32[8,8,8,254]{3,2,1,0:T(8,128)} %get-tuple-element.33) | copy-start | bytes 1560580
  194.9 3.2 %copy-start.9 = (f32[8,8,8,254]{3,2,1,0:T(8,128)S(1)}, f32[8,8,8,254]{3,2,1,0:T(8,128)}, u32[]{:S(2)}) copy-start(f32[8,8,8,254]{3,2,1,0:T(8,128)} %get-tuple-element.34) | copy-start | bytes 1560580
  194.9 3.3 %copy-start.10 = (f32[8,8,8,2]{3,2,1,0:T(8,128)S(1)}, f32[8,8,8,2]{3,2,1,0:T(8,128)}, u32[]{:S(2)}) copy-start(f32[8,8,8,2]{3,2,1,0:T(8,128)} %get-tuple-element.31) | copy-start | bytes 12292
  194.9 3.4 %copy-start.11 = (f32[8,8,8,2]{3,2,1,0:T(8,128)S(1)}, f32[8,8,8,2]{3,2,1,0:T(8,128)}, u32[]{:S(2)}) copy-start(f32[8,8,8,2]{3,2,1,0:T(8,128)} %get-tuple-element.32) | copy-start | bytes 12292
  194.9 3.4 %copy-start.12 = (f32[8,8,8,3]{3,2,1,0:T(8,128)S(1)}, f32[8,8,8,3]{3,2,1,0:T(8,128)}, u32[]{:S(2)}) copy-start(f32[8,8,8,3]{3,2,1,0:T(8,128)} %get-tuple-element.27) | copy-start | bytes 18436
  194.9 3.5 %copy-start.13 = (f32[8,8,8,3]{3,2,1,0:T(8,128)S(1)}, f32[8,8,8,3]{3,2,1,0:T(8,128)}, u32[]{:S(2)}) copy-start(f32[8,8,8,3]{3,2,1,0:T(8,128)} %get-tuple-element.28) | copy-start | bytes 18436
  194.9 3.6 %copy-start.14 = (f32[8,8,8,1]{3,2,1,0:T(8,128)S(1)}, f32[8,8,8,1]{3,2,1,0:T(8,128)}, u32[]{:S(2)}) copy-start(f32[8,8,8,1]{3,2,1,0:T(8,128)} %get-tuple-element.35) | copy-start | bytes 6148
  194.9 3.6 %copy-start.15 = (f32[8,8,8,1]{3,2,1,0:T(8,128)S(1)}, f32[8,8,8,1]{3,2,1,0:T(8,128)}, u32[]{:S(2)}) copy-start(f32[8,8,8,1]{3,2,1,0:T(8,128)} %get-tuple-element.36) | copy-start | bytes 6148
  198.5 1.0 copy-start.1
  198.6 1.2 copy-start.2
  198.6 1.4 copy-start.3
  202.3 3.4 %copy-start.16 = (f32[8,8,8,256]{3,2,1,0:T(8,128)S(1)}, f32[8,8,8,256]{3,2,1,0:T(8,128)}, u32[]{:S(2)}) copy-start(f32[8,8,8,256]{3,2,1,0:T(8,128)} %param.3) | copy-start | bytes 1572868
where the time goes:
time: 209 us
  blocking collectives  118 us (56%)
  starting transfers between devices  26.4 us (13%)
  waiting for transfers between devices  26.4 us (13%)
  other arithmetic  18.4 us (9%)
  local copies, waits for them, and re-layouts  16.6 us (8%)
  between operations  2.72 us (1%)
    pmax x1, blocking collectives, local(): fastest = lax.pmax(local_rate, ('gy', 'gz'))  118 us
    ppermute x2, waiting for transfers between devices, extended(): lax.ppermute(tail, axis, [(i, (i + 1) % count) for i in range(count)])  20 us
    ppermute x2, starting transfers between devices, extended(): lax.ppermute(head, axis, [((i + 1) % count, i) for i in range(count)])  15.8 us
    slice x18, local copies, waits for them, and re-layouts, rolled(): return jnp.roll(block, -step, axis=3)  14.3 us
    ppermute x2, starting transfers between devices, extended(): lax.ppermute(tail, axis, [(i, (i + 1) % count) for i in range(count)])  10.7 us
    ppermute x2, waiting for transfers between devices, extended(): lax.ppermute(head, axis, [((i + 1) % count, i) for i in range(count)])  6.33 us
    unnamed x7, other arithmetic  5.12 us
  transfers between devices with their start and end apart: 4, of which 4 were waited for; matrix products, arithmetic and copies ran while one was open for 3% of the time, Pallas kernels for 0%

commit v1 on v0

v1 whole, which is shorter than its diff:
```python
import jax
import jax.numpy as jnp
from jax import lax
from jax.experimental import pallas as pl
from jax.experimental.pallas import tpu as pltpu
from jax.sharding import PartitionSpec as P

MESH = pl.DeviceIdType.MESH
F32 = jnp.float32
MIXED = (2, 3, 6, 7)
X_SHIFT = 2
FAN = 32


def place():
    gy = lax.axis_index("gy")
    gz = lax.axis_index("gz")
    xs = lax.rem(gy // 2 + X_SHIFT, 8)
    y = lax.rem(gy, 2) * 4 + lax.rem(gz // 2, 4)
    return xs, y, gz // 8, lax.rem(gz, 2)


def device(xs, y, z, core):
    x = lax.rem(xs + 8 - X_SHIFT, 8)
    return (x * 2 + y // 4, (z * 4 + lax.rem(y, 4)) * 2 + core)


def member(leader, index):
    xs, y, core = leader
    return device(lax.rem(xs, 4) + 4 * (index // 16), lax.rem(y, 4) + 4 * lax.rem(index // 8, 2), lax.rem(index, 8), core)


ROOT = 17


def chief(index):
    at = lax.rem(index + ROOT, FAN)
    return device(at // 8, lax.rem(at // 2, 4), 0, lax.rem(at, 2))


def x_shift(t, s):
    return pltpu.roll(t, (256 - s) % 256, 1)


def y_shift(t, h, s):
    row = lax.broadcasted_iota(jnp.int32, t.shape, 0)
    if s > 0:
        return pltpu.roll(jnp.where(row < s, h, t), 8 - s, 0)
    return pltpu.roll(jnp.where(row >= 8 + s, h, t), -s, 0)


def first_of(f):
    return (
        (45.0 / 60.0) * (f(1) - f(-1))
        - (9.0 / 60.0) * (f(2) - f(-2))
        + (1.0 / 60.0) * (f(3) - f(-3))
    )


def second_of(f):
    return (
        (-490.0 / 180.0) * f(0)
        + (270.0 / 180.0) * (f(1) + f(-1))
        - (27.0 / 180.0) * (f(2) + f(-2))
        + (2.0 / 180.0) * (f(3) + f(-3))
    )


def memo(f):
    held = {}

    def get(s):
        if s not in held:
            held[s] = f(s)
        return held[s]

    return get


def along_x(t):
    return memo(lambda s: t if s == 0 else x_shift(t, s))


def substep(
    f_hbm,
    a_hbm,
    na_ref,
    top_ref,
    F,
    A,
    H,
    GY,
    B,
    J,
    own,
    ups,
    chiefs,
    down,
    load_sem,
    y_send,
    y_recv,
    z_send,
    z_recv,
    g_send,
    g_recv,
    t_send,
    t_recv,
):
    gy = lax.axis_index("gy")
    gz = lax.axis_index("gz")
    up_y, down_y = lax.rem(gy + 1, 16), lax.rem(gy + 15, 16)
    up_z, down_z = lax.rem(gz + 1, 64), lax.rem(gz + 63, 64)
    xs, y, z, core = place()
    in_group = (xs // 4) * 16 + (y // 4) * 8 + z
    among_chiefs = lax.rem(lax.rem(xs, 4) * 8 + lax.rem(y, 4) * 2 + core + FAN - ROOT, FAN)
    is_chief = in_group == 0
    is_root = jnp.logical_and(is_chief, among_chiefs == 0)
    group = (xs, y, core)

    load_f = pltpu.make_async_copy(f_hbm, F.at[:, pl.ds(3, 8)], load_sem.at[0])
    load_a = pltpu.make_async_copy(a_hbm, A, load_sem.at[1])
    load_f.start()
    load_a.start()

    barrier = pltpu.get_barrier_semaphore()
    for to in ((up_y, gz), (down_y, gz), (gy, up_z), (gy, down_z)):
        pl.semaphore_signal(barrier, inc=1, device_id=to, device_id_type=MESH)

    @pl.when(is_root)
    def _():
        def tell(i, c):
            pl.semaphore_signal(barrier, inc=1, device_id=chief(i), device_id_type=MESH)
            return c

        lax.fori_loop(0, FAN, tell, 0)

    @pl.when(is_chief)
    def _():
        def tell(i, c):
            pl.semaphore_signal(barrier, inc=1, device_id=member(group, i), device_id_type=MESH)
            return c

        lax.fori_loop(1, FAN, tell, 0)

    pl.semaphore_wait(barrier, 5)

    def remote(src, dst, send, recv, to):
        return pltpu.make_async_remote_copy(
            src_ref=src, dst_ref=dst, send_sem=send, recv_sem=recv, device_id=to, device_id_type=MESH
        )

    halos = []
    for part, (start, count) in enumerate(((5, 3), (0, 5))):
        ks = pl.ds(start, count)
        low, high = pl.ds(0, 3), pl.ds(5, 3)
        halos.append(
            [
                remote(f_hbm.at[ks, :, low], H.at[ks, :, low], y_send.at[0, part], y_recv.at[0, part], (down_y, gz)),
                remote(f_hbm.at[ks, :, high], H.at[ks, :, high], y_send.at[1, part], y_recv.at[1, part], (up_y, gz)),
                remote(f_hbm.at[ks, low], F.at[ks, pl.ds(11, 3)], z_send.at[0, part], z_recv.at[0, part], (gy, down_z)),
                remote(f_hbm.at[ks, high], F.at[ks, pl.ds(0, 3)], z_send.at[1, part], z_recv.at[1, part], (gy, up_z)),
            ]
        )
    for part in halos:
        for copy in part:
            copy.start()

    def along_y(k, i):
        t, h = F[k, i + 3], H[k, i]
        return memo(lambda s: t if s == 0 else y_shift(t, h, s))

    def along_z(k, i):
        return lambda s: F[k, i + 3 + s]

    load_f.wait()
    for copy in halos[0]:
        copy.wait_recv()

    own[...] = jnp.zeros_like(own)

    def rates(i, c):
        t = [F[k, i + 3] for k in range(8)]
        bx = first_of(along_y(7, i)) - first_of(along_z(6, i))
        by = first_of(along_z(5, i)) - first_of(along_x(t[7]))
        bz = first_of(along_x(t[6])) - first_of(along_y(5, i))
        B[0, i] = bx
        B[1, i] = by
        B[2, i] = bz
        cs2 = jnp.exp((5.0 / 3.0) * t[4] + (2.0 / 3.0) * t[0])
        inverse = jnp.exp(-t[0])
        rate = (
            jnp.abs(t[1])
            + jnp.abs(t[2])
            + jnp.abs(t[3])
            + jnp.sqrt(cs2 + (bx * bx + by * by + bz * bz) * inverse)
        )
        own[...] = jnp.maximum(own[...], jnp.maximum(rate[:, :128], rate[:, 128:]))
        return c

    lax.fori_loop(0, 8, rates, 0)

    to_chief = remote(own, ups.at[in_group], t_send.at[0], t_recv.at[0], member(group, 0))

    @pl.when(jnp.logical_not(is_chief))
    def _():
        to_chief.start()

    for copy in halos[1]:
        copy.wait_recv()

    def slopes(i, c):
        for j, k in enumerate(MIXED):
            GY[j, i + 3] = first_of(along_y(k, i))
        return c

    lax.fori_loop(0, 8, slopes, 0)
    edges = [
        remote(GY.at[:, pl.ds(3, 3)], GY.at[:, pl.ds(11, 3)], g_send.at[0], g_recv.at[0], (gy, down_z)),
        remote(GY.at[:, pl.ds(8, 3)], GY.at[:, pl.ds(0, 3)], g_send.at[1], g_recv.at[1], (gy, up_z)),
    ]
    for copy in edges:
        copy.start()
    load_a.wait()

    def partial(i, c):
        t = [F[k, i + 3] for k in range(8)]
        ax = [along_x(t[k]) for k in range(8)]
        ay = [along_y(k, i) for k in range(8)]
        az = [along_z(k, i) for k in range(8)]
        dx = {k: first_of(ax[k]) for k in range(5)}
        dy = {k: GY[MIXED.index(k), i + 3] if k in MIXED else first_of(ay[k]) for k in range(7)}
        dz = {k: first_of(az[k]) for k in (0, 1, 2, 3, 4, 5, 7)}
        u = t[1:4]
        bx, by, bz = B[0, i], B[1, i], B[2, i]

        def put(k, value):
            na_ref[k, i] = (-5.0 / 9.0) * A[k, i] + value

        def advect(k):
            return u[0] * dx[k] + u[1] * dy[k] + u[2] * dz[k]

        divu = dx[1] + dy[2] + dz[3]
        third = divu * (1.0 / 3.0)
        sxx, syy, szz = dx[1] - third, dy[2] - third, dz[3] - third
        sxy = 0.5 * (dy[1] + dx[2])
        sxz = 0.5 * (dz[1] + dx[3])
        syz = 0.5 * (dz[2] + dy[3])
        cs2 = jnp.exp((5.0 / 3.0) * t[4] + (2.0 / 3.0) * t[0])
        put(0, -advect(0) - divu)
        strain = ((sxx, sxy, sxz), (sxy, syy, syz), (sxz, syz, szz))
        xx = second_of(ax[1]), second_of(ax[2]), second_of(ax[3])
        yy = second_of(ay[1]), second_of(ay[2]), second_of(ay[3])
        zz = second_of(az[1]), second_of(az[2]), second_of(az[3])
        mixed = (
            xx[0] + first_of(along_x(dy[2])) + first_of(along_x(dz[3])),
            yy[1] + first_of(along_x(dy[1])),
            zz[2] + first_of(along_x(dz[1])),
        )
        grad = (dx, dy, dz)
        for n in range(3):
            viscous = (
                xx[n]
                + yy[n]
                + zz[n]
                + mixed[n] * (1.0 / 3.0)
                + 2.0 * (strain[n][0] * dx[0] + strain[n][1] * dy[0] + strain[n][2] * dz[0])
            )
            put(1 + n, -advect(1 + n) - cs2 * (grad[n][4] + grad[n][0]) + 0.1 * viscous)
        norm = sxx * sxx + syy * syy + szz * szz + 2.0 * (sxy * sxy + sxz * sxz + syz * syz)
        put(4, -advect(4) + 0.2 * norm / (1.5 * cs2))

        xx = second_of(ax[5]), second_of(ax[6]), second_of(ax[7])
        yy = second_of(ay[5]), second_of(ay[6]), second_of(ay[7])
        zz = second_of(az[5]), second_of(az[6]), second_of(az[7])
        J[0, i] = first_of(along_x(dy[6])) + first_of(along_x(dz[7])) - yy[0] - zz[0]
        J[1, i] = first_of(along_x(dy[5])) - xx[1] - zz[1]
        J[2, i] = first_of(along_x(dz[5])) - xx[2] - yy[2]
        cross = (u[1] * bz - u[2] * by, u[2] * bx - u[0] * bz, u[0] * by - u[1] * bx)
        for n in range(3):
            put(5 + n, cross[n] + 0.1 * (xx[n] + yy[n] + zz[n]))
        return c

    lax.fori_loop(0, 8, partial, 0)

    for copy in edges:
        copy.wait_recv()

    def finish(i, c):
        yz = [first_of(lambda s, j=j: GY[j, i + 3 + s]) for j in range(4)]
        bx, by, bz = B[0, i], B[1, i], B[2, i]
        jx, jy, jz = J[0, i], J[1, i] + yz[3], J[2, i] + yz[2]
        inverse = jnp.exp(-F[0, i + 3])
        cs2 = jnp.exp((5.0 / 3.0) * F[4, i + 3] + (2.0 / 3.0) * F[0, i + 3])
        na_ref[1, i] = na_ref[1, i] + (jy * bz - jz * by) * inverse
        na_ref[2, i] = na_ref[2, i] + (jz * bx - jx * bz) * inverse + (0.1 / 3.0) * yz[1]
        na_ref[3, i] = na_ref[3, i] + (jx * by - jy * bx) * inverse + (0.1 / 3.0) * yz[0]
        na_ref[4, i] = na_ref[4, i] + 0.1 * (jx * jx + jy * jy + jz * jz) * inverse / (1.5 * cs2)
        return c

    lax.fori_loop(0, 8, finish, 0)

    to_root = remote(own, chiefs.at[among_chiefs], t_send.at[1], t_recv.at[1], chief(0))
    all_ups = remote(ups.at[pl.ds(1, FAN - 1)], ups.at[pl.ds(1, FAN - 1)], t_send.at[2], t_recv.at[0], chief(0))
    all_chiefs = remote(chiefs.at[pl.ds(1, FAN - 1)], chiefs.at[pl.ds(1, FAN - 1)], t_send.at[3], t_recv.at[1], chief(0))
    to_down = remote(down, down, t_send.at[2], t_recv.at[2], chief(0))

    @pl.when(is_chief)
    def _():
        all_ups.wait_recv()
        own[...] = jnp.maximum(own[...], jnp.max(ups[1:], axis=0))

        @pl.when(jnp.logical_not(is_root))
        def _():
            to_root.start()

    @pl.when(is_root)
    def _():
        all_chiefs.wait_recv()
        most = jnp.max(jnp.maximum(own[...], jnp.max(chiefs[1:], axis=0)))
        down[...] = jnp.full(down.shape, most, F32)

        def tell(i, c):
            remote(down, down, t_send.at[3], t_recv.at[2], chief(i)).start()
            return c

        lax.fori_loop(1, FAN, tell, 0)

    @pl.when(jnp.logical_not(is_root))
    def _():
        to_down.wait_recv()

    @pl.when(is_chief)
    def _():
        def tell(i, c):
            remote(down, down, t_send.at[2], t_recv.at[2], member(group, i)).start()
            return c

        lax.fori_loop(1, FAN, tell, 0)

    top_ref[...] = down[...]

    for part in halos:
        for copy in part:
            copy.wait_send()
    for copy in edges:
        copy.wait_send()

    @pl.when(jnp.logical_not(is_chief))
    def _():
        to_chief.wait_send()

    @pl.when(is_chief)
    def _():
        all_ups.wait_send()

        @pl.when(jnp.logical_not(is_root))
        def _():
            to_root.wait_send()

    @pl.when(is_root)
    def _():
        all_chiefs.wait_send()


def update(f_ref, na_ref, top_ref, nf_ref, out_ref, dt_ref):
    dt = 0.4 / top_ref[...]
    dt_ref[0] = dt[0, 0]
    scale = (15.0 / 16.0) * dt[0:1, 0:1]
    na = na_ref[...]
    out_ref[...] = na
    nf_ref[...] = f_ref[...] + scale[None, None] * na


def local(fields, accum):
    block = jax.ShapeDtypeStruct(fields.shape, F32)
    vmem = pl.BlockSpec(memory_space=pltpu.VMEM)
    anywhere = pl.BlockSpec(memory_space=pl.ANY)
    na, top = pl.pallas_call(
        substep,
        out_shape=(block, jax.ShapeDtypeStruct((8, 128), F32)),
        in_specs=[anywhere, anywhere],
        out_specs=(vmem, vmem),
        scratch_shapes=[
            pltpu.VMEM((8, 14, 8, 256), F32),
            pltpu.VMEM((8, 8, 8, 256), F32),
            pltpu.VMEM((8, 8, 8, 256), F32),
            pltpu.VMEM((4, 14, 8, 256), F32),
            pltpu.VMEM((3, 8, 8, 256), F32),
            pltpu.VMEM((3, 8, 8, 256), F32),
            pltpu.VMEM((8, 128), F32),
            pltpu.VMEM((FAN, 8, 128), F32),
            pltpu.VMEM((FAN, 8, 128), F32),
            pltpu.VMEM((8, 128), F32),
            pltpu.SemaphoreType.DMA((2,)),
            pltpu.SemaphoreType.DMA((2, 2)),
            pltpu.SemaphoreType.DMA((2, 2)),
            pltpu.SemaphoreType.DMA((2, 2)),
            pltpu.SemaphoreType.DMA((2, 2)),
            pltpu.SemaphoreType.DMA((2,)),
            pltpu.SemaphoreType.DMA((2,)),
            pltpu.SemaphoreType.DMA((4,)),
            pltpu.SemaphoreType.DMA((3,)),
        ],
        compiler_params=pltpu.CompilerParams(
            collective_id=0, has_side_effects=True, vmem_limit_bytes=60 * 1024 * 1024
        ),
        cost_estimate=pl.CostEstimate(flops=13_000_000, bytes_accessed=2_000_000, transcendentals=100_000),
    )(fields, accum)
    return pl.pallas_call(
        update,
        out_shape=(block, block, jax.ShapeDtypeStruct((1,), F32)),
        in_specs=[vmem, vmem, vmem],
        out_specs=(vmem, vmem, pl.BlockSpec(memory_space=pltpu.SMEM)),
        compiler_params=pltpu.CompilerParams(vmem_limit_bytes=32 * 1024 * 1024),
        cost_estimate=pl.CostEstimate(flops=300_000, bytes_accessed=2_500_000, transcendentals=0),
    )(fields, na, top)


def solution(mesh):
    in_specs = (P(None, "gz", "gy", None), P(None, "gz", "gy", None))
    out_specs = (P(None, "gz", "gy", None), P(None, "gz", "gy", None), P())
    return jax.shard_map(local, mesh=mesh, in_specs=in_specs, out_specs=out_specs, check_vma=False)
```

time: 209 us -> 70.4 us (0.34)
  the two profiles are of different devices: /device:TPU:1 before, /device:TPU:118 now
where the time goes in v1:
time: 70.4 us; the launch traced here: 70.2 us
  Pallas kernels  67.8 us (96%)
  local copies, waits for them, and re-layouts  1.72 us (2%)
    pallas_call x1, Pallas kernels, local(): pl.pallas_call(substep, out_shape=(block, jax.ShapeDtypeStruct((8, 128),...  66.7 us
    unnamed x6, local copies, waits for them, and re-layouts  1.72 us

profile of v1, /device:TPU:118, one launch (start us, length us, event | category | flops | bytes accessed | tf_op | source)
XLA Modules:
  0.0 70.2 jit_solution(18225179620912343163)
XLA Ops:
  0.6 0.0 copy-start
  0.6 66.7 %shard_map.49 = (f32[8,8,8,256]{3,2,1,0:T(8,128)}, f32[8,128]{1,0:T(8,128)}) custom-call(f32[8,8,8,256]{3,2,1,0:T(8,128)} %f_ref.1, f32[8,8,8,256]{3,2,1,0:T(8,128)} %a_hbm.1), custom_call_target="tpu_custom_call" | custom-call | flops 13000000 | bytes 2000000 | tf_op jit(solution)/shard_map/pallas_call | solution.py:378
  67.4 0.0 copy-done
  67.4 0.0 copy-start.1
  67.4 1.0 %copy-done.1 = f32[8,8,8,256]{3,2,1,0:T(8,128)S(1)} copy-done((f32[8,8,8,256]{3,2,1,0:T(8,128)S(1)}, f32[8,8,8,256]{3,2,1,0:T(8,128)}, u32[]{:S(2)}) %copy-start.1) | copy-done | bytes 524312
  68.4 0.0 copy-start.2
  68.4 0.7 copy-done.2
  69.1 1.0 %shard_map.50 = (f32[8,8,8,256]{3,2,1,0:T(8,128)}, f32[8,8,8,256]{3,2,1,0:T(8,128)}, f32[1]{0:T(128)}) custom-call(f32[8,8,8,256]{3,2,1,0:T(8,128)S(1)} %copy-done, f32[8,8,8,256]{3,2,1,0:T(8,128)S(1)} %copy-done.1, f32[8,128]{1,0:T(8,128)S(1)} %copy-done.2), custom_call_target="tpu_custom_call" | custom-call | flops 300000 | bytes 2500000 | tf_op jit(solution)/shard_map/pallas_call | solution.py:409
Async XLA Ops:
  0.6 66.8 %copy-start = (f32[8,8,8,256]{3,2,1,0:T(8,128)S(1)}, f32[8,8,8,256]{3,2,1,0:T(8,128)}, u32[]{:S(2)}) copy-start(f32[8,8,8,256]{3,2,1,0:T(8,128)} %f_ref.1) | copy-start | bytes 1572868
  67.4 1.0 %copy-start.1 = (f32[8,8,8,256]{3,2,1,0:T(8,128)S(1)}, f32[8,8,8,256]{3,2,1,0:T(8,128)}, u32[]{:S(2)}) copy-start(f32[8,8,8,256]{3,2,1,0:T(8,128)} %get-tuple-element.5.na_ref) | copy-start | bytes 1572868
  68.4 0.7 copy-start.2

commit v2 on v1

--- a/solution.py
+++ b/solution.py
@@ -8,34 +8,22 @@
 MESH = pl.DeviceIdType.MESH
 F32 = jnp.float32
 MIXED = (2, 3, 6, 7)
-X_SHIFT = 2
-FAN = 32
-
-
-def place():
-    gy = lax.axis_index("gy")
-    gz = lax.axis_index("gz")
-    xs = lax.rem(gy // 2 + X_SHIFT, 8)
-    y = lax.rem(gy, 2) * 4 + lax.rem(gz // 2, 4)
-    return xs, y, gz // 8, lax.rem(gz, 2)
-
-
-def device(xs, y, z, core):
-    x = lax.rem(xs + 8 - X_SHIFT, 8)
-    return (x * 2 + y // 4, (z * 4 + lax.rem(y, 4)) * 2 + core)
-
-
-def member(leader, index):
-    xs, y, core = leader
-    return device(lax.rem(xs, 4) + 4 * (index // 16), lax.rem(y, 4) + 4 * lax.rem(index // 8, 2), lax.rem(index, 8), core)
-
-
-ROOT = 17
+COLUMN = 8
+PLANE = 128
 
 
 def chief(index):
-    at = lax.rem(index + ROOT, FAN)
-    return device(at // 8, lax.rem(at // 2, 4), 0, lax.rem(at, 2))
+    at = (index + 1) % PLANE
+    return at // 8, at % 8
+
+
+def hops(index):
+    gy, gz = chief(index)
+    x, y = gy // 2, gy % 2 * 4 + gz // 2
+    return min(x, 8 - x) + min(y, 8 - y)
+
+
+NEAR_FIRST = sorted(range(1, PLANE), key=hops)
 
 
 def x_shift(t, s):
@@ -92,6 +80,7 @@
     GY,
     B,
     J,
+    tile,
     own,
     ups,
     chiefs,
@@ -110,12 +99,10 @@
     gz = lax.axis_index("gz")
     up_y, down_y = lax.rem(gy + 1, 16), lax.rem(gy + 15, 16)
     up_z, down_z = lax.rem(gz + 1, 64), lax.rem(gz + 63, 64)
-    xs, y, z, core = place()
-    in_group = (xs // 4) * 16 + (y // 4) * 8 + z
-    among_chiefs = lax.rem(lax.rem(xs, 4) * 8 + lax.rem(y, 4) * 2 + core + FAN - ROOT, FAN)
-    is_chief = in_group == 0
-    is_root = jnp.logical_and(is_chief, among_chiefs == 0)
-    group = (xs, y, core)
+    level = gz // 8
+    among = lax.rem(gy * 8 + gz + PLANE - 1, PLANE)
+    is_chief = level == 0
+    is_root = jnp.logical_and(gy == 0, gz == 1)
 
     load_f = pltpu.make_async_copy(f_hbm, F.at[:, pl.ds(3, 8)], load_sem.at[0])
     load_a = pltpu.make_async_copy(a_hbm, A, load_sem.at[1])
@@ -128,19 +115,13 @@
 
     @pl.when(is_root)
     def _():
-        def tell(i, c):
+        for i in [0, *NEAR_FIRST]:
             pl.semaphore_signal(barrier, inc=1, device_id=chief(i), device_id_type=MESH)
-            return c
-
-        lax.fori_loop(0, FAN, tell, 0)
 
     @pl.when(is_chief)
     def _():
-        def tell(i, c):
-            pl.semaphore_signal(barrier, inc=1, device_id=member(group, i), device_id_type=MESH)
-            return c
-
-        lax.fori_loop(1, FAN, tell, 0)
+        for i in range(1, COLUMN):
+            pl.semaphore_signal(barrier, inc=1, device_id=(gy, gz + 8 * i), device_id_type=MESH)
 
     pl.semaphore_wait(barrier, 5)
 
@@ -149,21 +130,32 @@
             src_ref=src, dst_ref=dst, send_sem=send, recv_sem=recv, device_id=to, device_id_type=MESH
         )
 
-    halos = []
-    for part, (start, count) in enumerate(((5, 3), (0, 5))):
+    low, high = pl.ds(0, 3), pl.ds(5, 3)
+
+    def y_halo(part, start, count):
         ks = pl.ds(start, count)
-        low, high = pl.ds(0, 3), pl.ds(5, 3)
-        halos.append(
-            [
-                remote(f_hbm.at[ks, :, low], H.at[ks, :, low], y_send.at[0, part], y_recv.at[0, part], (down_y, gz)),
-                remote(f_hbm.at[ks, :, high], H.at[ks, :, high], y_send.at[1, part], y_recv.at[1, part], (up_y, gz)),
-                remote(f_hbm.at[ks, low], F.at[ks, pl.ds(11, 3)], z_send.at[0, part], z_recv.at[0, part], (gy, down_z)),
-                remote(f_hbm.at[ks, high], F.at[ks, pl.ds(0, 3)], z_send.at[1, part], z_recv.at[1, part], (gy, up_z)),
-            ]
-        )
-    for part in halos:
-        for copy in part:
-            copy.start()
+        return [
+            remote(f_hbm.at[ks, :, low], H.at[ks, :, low], y_send.at[0, part], y_recv.at[0, part], (down_y, gz)),
+            remote(f_hbm.at[ks, :, high], H.at[ks, :, high], y_send.at[1, part], y_recv.at[1, part], (up_y, gz)),
+        ]
+
+    def z_halo(part, start, count):
+        ks = pl.ds(start, count)
+        return [
+            remote(f_hbm.at[ks, low], F.at[ks, pl.ds(11, 3)], z_send.at[0, part], z_recv.at[0, part], (gy, down_z)),
+            remote(f_hbm.at[ks, high], F.at[ks, pl.ds(0, 3)], z_send.at[1, part], z_recv.at[1, part], (gy, up_z)),
+        ]
+
+    first = y_halo(0, 5, 1) + y_halo(1, 7, 1) + z_halo(0, 5, 2)
+    then_y = y_halo(2, 6, 1) + y_halo(3, 2, 2)
+    then_z = z_halo(1, 7, 1) + z_halo(2, 0, 5)
+    last_y = y_halo(4, 0, 2) + y_halo(5, 4, 1)
+    for copy in first + then_z:
+        copy.start()
+    for copy in first:
+        copy.wait_send()
+    for copy in then_y:
+        copy.start()
 
     def along_y(k, i):
         t, h = F[k, i + 3], H[k, i]
@@ -173,10 +165,10 @@
         return lambda s: F[k, i + 3 + s]
 
     load_f.wait()
-    for copy in halos[0]:
+    for copy in first:
         copy.wait_recv()
 
-    own[...] = jnp.zeros_like(own)
+    tile[...] = jnp.zeros_like(tile)
 
     def rates(i, c):
         t = [F[k, i + 3] for k in range(8)]
@@ -194,18 +186,33 @@
             + jnp.abs(t[3])
             + jnp.sqrt(cs2 + (bx * bx + by * by + bz * bz) * inverse)
         )
-        own[...] = jnp.maximum(own[...], jnp.maximum(rate[:, :128], rate[:, 128:]))
+        tile[...] = jnp.maximum(tile[...], jnp.maximum(rate[:, :128], rate[:, 128:]))
         return c
 
     lax.fori_loop(0, 8, rates, 0)
 
-    to_chief = remote(own, ups.at[in_group], t_send.at[0], t_recv.at[0], member(group, 0))
+    own[...] = jnp.max(tile[...], axis=0, keepdims=True)
+    chief_id = (gy, lax.rem(gz, 8))
+    to_chief = remote(own, ups.at[level], t_send.at[0], t_recv.at[0], chief_id)
+    all_ups = remote(ups.at[pl.ds(1, COLUMN - 1)], ups.at[pl.ds(1, COLUMN - 1)], t_send.at[2], t_recv.at[0], chief_id)
+    to_root = remote(own, chiefs.at[among], t_send.at[1], t_recv.at[1], chief(0))
+    all_chiefs = remote(chiefs.at[pl.ds(1, PLANE - 1)], chiefs.at[pl.ds(1, PLANE - 1)], t_send.at[3], t_recv.at[1], chief(0))
+    to_down = remote(down, down, t_send.at[2], t_recv.at[2], chief(0))
 
     @pl.when(jnp.logical_not(is_chief))
     def _():
         to_chief.start()
 
-    for copy in halos[1]:
+    @pl.when(is_chief)
+    def _():
+        all_ups.wait_recv()
+        own[...] = jnp.maximum(own[...], jnp.max(ups[1:], axis=0))
+
+        @pl.when(jnp.logical_not(is_root))
+        def _():
+            to_root.start()
+
+    for copy in then_y:
         copy.wait_recv()
 
     def slopes(i, c):
@@ -218,9 +225,11 @@
         remote(GY.at[:, pl.ds(3, 3)], GY.at[:, pl.ds(11, 3)], g_send.at[0], g_recv.at[0], (gy, down_z)),
         remote(GY.at[:, pl.ds(8, 3)], GY.at[:, pl.ds(0, 3)], g_send.at[1], g_recv.at[1], (gy, up_z)),
     ]
-    for copy in edges:
+    for copy in edges + last_y:
         copy.start()
     load_a.wait()
+    for copy in then_z + last_y:
+        copy.wait_recv()
 
     def partial(i, c):
         t = [F[k, i + 3] for k in range(8)]
@@ -299,31 +308,13 @@
 
     lax.fori_loop(0, 8, finish, 0)
 
-    to_root = remote(own, chiefs.at[among_chiefs], t_send.at[1], t_recv.at[1], chief(0))
-    all_ups = remote(ups.at[pl.ds(1, FAN - 1)], ups.at[pl.ds(1, FAN - 1)], t_send.at[2], t_recv.at[0], chief(0))
-    all_chiefs = remote(chiefs.at[pl.ds(1, FAN - 1)], chiefs.at[pl.ds(1, FAN - 1)], t_send.at[3], t_recv.at[1], chief(0))
-    to_down = remote(down, down, t_send.at[2], t_recv.at[2], chief(0))
-
-    @pl.when(is_chief)
-    def _():
-        all_ups.wait_recv()
-        own[...] = jnp.maximum(own[...], jnp.max(ups[1:], axis=0))
-
-        @pl.when(jnp.logical_not(is_root))
-        def _():
-            to_root.start()
-
     @pl.when(is_root)
     def _():
         all_chiefs.wait_recv()
         most = jnp.max(jnp.maximum(own[...], jnp.max(chiefs[1:], axis=0)))
         down[...] = jnp.full(down.shape, most, F32)
-
-        def tell(i, c):
+        for i in NEAR_FIRST:
             remote(down, down, t_send.at[3], t_recv.at[2], chief(i)).start()
-            return c
-
-        lax.fori_loop(1, FAN, tell, 0)
 
     @pl.when(jnp.logical_not(is_root))
     def _():
@@ -331,18 +322,12 @@
 
     @pl.when(is_chief)
     def _():
-        def tell(i, c):
-            remote(down, down, t_send.at[2], t_recv.at[2], member(group, i)).start()
-            return c
-
-        lax.fori_loop(1, FAN, tell, 0)
+        for i in range(1, COLUMN):
+            remote(down, down, t_send.at[2], t_recv.at[2], (gy, gz + 8 * i)).start()
 
     top_ref[...] = down[...]
 
-    for part in halos:
-        for copy in part:
-            copy.wait_send()
-    for copy in edges:
+    for copy in then_y + then_z + last_y + edges:
         copy.wait_send()
 
     @pl.when(jnp.logical_not(is_chief))
@@ -365,7 +350,7 @@
 def update(f_ref, na_ref, top_ref, nf_ref, out_ref, dt_ref):
     dt = 0.4 / top_ref[...]
     dt_ref[0] = dt[0, 0]
-    scale = (15.0 / 16.0) * dt[0:1, 0:1]
+    scale = (15.0 / 16.0) * dt[:, 0:1]
     na = na_ref[...]
     out_ref[...] = na
     nf_ref[...] = f_ref[...] + scale[None, None] * na
@@ -377,7 +362,7 @@
     anywhere = pl.BlockSpec(memory_space=pl.ANY)
     na, top = pl.pallas_call(
         substep,
-        out_shape=(block, jax.ShapeDtypeStruct((8, 128), F32)),
+        out_shape=(pltpu.VMEM(fields.shape, F32), pltpu.VMEM((1, 128), F32)),
         in_specs=[anywhere, anywhere],
         out_specs=(vmem, vmem),
         scratch_shapes=[
@@ -388,14 +373,15 @@
             pltpu.VMEM((3, 8, 8, 256), F32),
             pltpu.VMEM((3, 8, 8, 256), F32),
             pltpu.VMEM((8, 128), F32),
-            pltpu.VMEM((FAN, 8, 128), F32),
-            pltpu.VMEM((FAN, 8, 128), F32),
-            pltpu.VMEM((8, 128), F32),
+            pltpu.VMEM((1, 128), F32),
+            pltpu.VMEM((COLUMN, 1, 128), F32),
+            pltpu.VMEM((PLANE, 1, 128), F32),
+            pltpu.VMEM((1, 128), F32),
             pltpu.SemaphoreType.DMA((2,)),
-            pltpu.SemaphoreType.DMA((2, 2)),
-            pltpu.SemaphoreType.DMA((2, 2)),
-            pltpu.SemaphoreType.DMA((2, 2)),
-            pltpu.SemaphoreType.DMA((2, 2)),
+            pltpu.SemaphoreType.DMA((2, 6)),
+            pltpu.SemaphoreType.DMA((2, 6)),
+            pltpu.SemaphoreType.DMA((2, 3)),
+            pltpu.SemaphoreType.DMA((2, 3)),
             pltpu.SemaphoreType.DMA((2,)),
             pltpu.SemaphoreType.DMA((2,)),
             pltpu.SemaphoreType.DMA((4,)),

time: 70.4 us -> 52 us (0.74)
  the two profiles are of different devices: /device:TPU:118 before, /device:TPU:16 now
where the time goes in v2:
time: 52 us; the launch traced here: 51.9 us
  Pallas kernels  51.2 us (98%)
  between operations  0.65 us (1%)
    pallas_call x1, Pallas kernels, local(): pl.pallas_call(substep, out_shape=(pltpu.VMEM(fields.shape, F32), pltpu.V...  50.2 us

profile of v2, /device:TPU:16, one launch (start us, length us, event | category | flops | bytes accessed | tf_op | source)
XLA Modules:
  0.0 51.9 jit_solution(16639087611544241311)
XLA Ops:
  0.6 0.0 copy-start
  0.6 50.2 %shard_map.49 = (f32[8,8,8,256]{3,2,1,0:T(8,128)S(1)}, f32[1,128]{1,0:T(1,128)S(1)}) custom-call(f32[8,8,8,256]{3,2,1,0:T(8,128)} %f_ref.1, f32[8,8,8,256]{3,2,1,0:T(8,128)} %a_hbm.1), custom_call_target="tpu_custom_call" | custom-call | flops 13000000 | bytes 2000000 | tf_op jit(solution)/shard_map/pallas_call | solution.py:363
  50.8 0.0 copy-done
  50.8 1.0 %shard_map.50 = (f32[8,8,8,256]{3,2,1,0:T(8,128)}, f32[8,8,8,256]{3,2,1,0:T(8,128)}, f32[1]{0:T(128)}) custom-call(f32[8,8,8,256]{3,2,1,0:T(8,128)S(1)} %copy-done, f32[8,8,8,256]{3,2,1,0:T(8,128)S(1)} %get-tuple-element.5.na_ref, f32[1,128]{1,0:T(1,128)S(1)} %get-tuple-element.6.top_ref), custom_call_target="tpu_custom_call" | custom-call | flops 300000 | bytes 2500000 | tf_op jit(solution)/shard_map/pallas_call | solution.py:395
Async XLA Ops:
  0.6 50.2 %copy-start = (f32[8,8,8,256]{3,2,1,0:T(8,128)S(1)}, f32[8,8,8,256]{3,2,1,0:T(8,128)}, u32[]{:S(2)}) copy-start(f32[8,8,8,256]{3,2,1,0:T(8,128)} %f_ref.1) | copy-start | bytes 1572868

commit v3 on v2

--- a/solution.py
+++ b/solution.py
@@ -79,7 +79,6 @@
     H,
     GY,
     B,
-    J,
     tile,
     own,
     ups,
@@ -90,8 +89,8 @@
     y_recv,
     z_send,
     z_recv,
-    g_send,
-    g_recv,
+    c_send,
+    c_recv,
     t_send,
     t_recv,
 ):
@@ -135,8 +134,8 @@
     def y_halo(part, start, count):
         ks = pl.ds(start, count)
         return [
-            remote(f_hbm.at[ks, :, low], H.at[ks, :, low], y_send.at[0, part], y_recv.at[0, part], (down_y, gz)),
-            remote(f_hbm.at[ks, :, high], H.at[ks, :, high], y_send.at[1, part], y_recv.at[1, part], (up_y, gz)),
+            remote(f_hbm.at[ks, :, low], H.at[ks, pl.ds(3, 8), low], y_send.at[0, part], y_recv.at[0, part], (down_y, gz)),
+            remote(f_hbm.at[ks, :, high], H.at[ks, pl.ds(3, 8), high], y_send.at[1, part], y_recv.at[1, part], (up_y, gz)),
         ]
 
     def z_halo(part, start, count):
@@ -146,19 +145,24 @@
             remote(f_hbm.at[ks, high], F.at[ks, pl.ds(0, 3)], z_send.at[1, part], z_recv.at[1, part], (gy, up_z)),
         ]
 
+    def corner(part, start):
+        ks, near, far = pl.ds(start, 2), pl.ds(0, 3), pl.ds(11, 3)
+        return [
+            remote(F.at[ks, near, low], H.at[ks, near, low], c_send.at[0, part], c_recv.at[0, part], (down_y, gz)),
+            remote(F.at[ks, near, high], H.at[ks, near, high], c_send.at[1, part], c_recv.at[1, part], (up_y, gz)),
+            remote(F.at[ks, far, low], H.at[ks, far, low], c_send.at[2, part], c_recv.at[2, part], (down_y, gz)),
+            remote(F.at[ks, far, high], H.at[ks, far, high], c_send.at[3, part], c_recv.at[3, part], (up_y, gz)),
+        ]
+
     first = y_halo(0, 5, 1) + y_halo(1, 7, 1) + z_halo(0, 5, 2)
-    then_y = y_halo(2, 6, 1) + y_halo(3, 2, 2)
     then_z = z_halo(1, 7, 1) + z_halo(2, 0, 5)
-    last_y = y_halo(4, 0, 2) + y_halo(5, 4, 1)
+    then_y = y_halo(2, 6, 1) + y_halo(3, 0, 5)
+    corners = corner(0, 2) + corner(1, 6)
     for copy in first + then_z:
         copy.start()
-    for copy in first:
-        copy.wait_send()
-    for copy in then_y:
-        copy.start()
 
     def along_y(k, i):
-        t, h = F[k, i + 3], H[k, i]
+        t, h = F[k, i + 3], H[k, i + 3]
         return memo(lambda s: t if s == 0 else y_shift(t, h, s))
 
     def along_z(k, i):
@@ -203,6 +207,17 @@
     def _():
         to_chief.start()
 
+    for copy in then_y:
+        copy.start()
+
+    def forward():
+        for copy in then_z:
+            copy.wait_recv()
+        for copy in corners:
+            copy.start()
+
+    pl.when(gz != 0)(forward)
+
     @pl.when(is_chief)
     def _():
         all_ups.wait_recv()
@@ -212,24 +227,18 @@
         def _():
             to_root.start()
 
-    for copy in then_y:
+    pl.when(gz == 0)(forward)
+
+    load_a.wait()
+    for copy in then_y + corners:
         copy.wait_recv()
 
     def slopes(i, c):
         for j, k in enumerate(MIXED):
-            GY[j, i + 3] = first_of(along_y(k, i))
+            GY[j, i] = first_of(along_y(k, i - 3))
         return c
 
-    lax.fori_loop(0, 8, slopes, 0)
-    edges = [
-        remote(GY.at[:, pl.ds(3, 3)], GY.at[:, pl.ds(11, 3)], g_send.at[0], g_recv.at[0], (gy, down_z)),
-        remote(GY.at[:, pl.ds(8, 3)], GY.at[:, pl.ds(0, 3)], g_send.at[1], g_recv.at[1], (gy, up_z)),
-    ]
-    for copy in edges + last_y:
-        copy.start()
-    load_a.wait()
-    for copy in then_z + last_y:
-        copy.wait_recv()
+    lax.fori_loop(0, 14, slopes, 0)
 
     def partial(i, c):
         t = [F[k, i + 3] for k in range(8)]
@@ -241,6 +250,8 @@
         dz = {k: first_of(az[k]) for k in (0, 1, 2, 3, 4, 5, 7)}
         u = t[1:4]
         bx, by, bz = B[0, i], B[1, i], B[2, i]
+        yz = [first_of(lambda s, j=j: GY[j, i + 3 + s]) for j in range(4)]
+        inverse = jnp.exp(-t[0])
 
         def put(k, value):
             na_ref[k, i] = (-5.0 / 9.0) * A[k, i] + value
@@ -257,13 +268,20 @@
         cs2 = jnp.exp((5.0 / 3.0) * t[4] + (2.0 / 3.0) * t[0])
         put(0, -advect(0) - divu)
         strain = ((sxx, sxy, sxz), (sxy, syy, syz), (sxz, syz, szz))
+        axx = second_of(ax[5]), second_of(ax[6]), second_of(ax[7])
+        ayy = second_of(ay[5]), second_of(ay[6]), second_of(ay[7])
+        azz = second_of(az[5]), second_of(az[6]), second_of(az[7])
+        jx = first_of(along_x(dy[6])) + first_of(along_x(dz[7])) - ayy[0] - azz[0]
+        jy = first_of(along_x(dy[5])) + yz[3] - axx[1] - azz[1]
+        jz = first_of(along_x(dz[5])) + yz[2] - axx[2] - ayy[2]
+        lorentz = (jy * bz - jz * by, jz * bx - jx * bz, jx * by - jy * bx)
         xx = second_of(ax[1]), second_of(ax[2]), second_of(ax[3])
         yy = second_of(ay[1]), second_of(ay[2]), second_of(ay[3])
         zz = second_of(az[1]), second_of(az[2]), second_of(az[3])
         mixed = (
             xx[0] + first_of(along_x(dy[2])) + first_of(along_x(dz[3])),
-            yy[1] + first_of(along_x(dy[1])),
-            zz[2] + first_of(along_x(dz[1])),
+            yy[1] + first_of(along_x(dy[1])) + yz[1],
+            zz[2] + first_of(along_x(dz[1])) + yz[0],
         )
         grad = (dx, dy, dz)
         for n in range(3):
@@ -274,39 +292,20 @@
                 + mixed[n] * (1.0 / 3.0)
                 + 2.0 * (strain[n][0] * dx[0] + strain[n][1] * dy[0] + strain[n][2] * dz[0])
             )
-            put(1 + n, -advect(1 + n) - cs2 * (grad[n][4] + grad[n][0]) + 0.1 * viscous)
+            put(
+                1 + n,
+                -advect(1 + n) - cs2 * (grad[n][4] + grad[n][0]) + lorentz[n] * inverse + 0.1 * viscous,
+            )
         norm = sxx * sxx + syy * syy + szz * szz + 2.0 * (sxy * sxy + sxz * sxz + syz * syz)
-        put(4, -advect(4) + 0.2 * norm / (1.5 * cs2))
-
-        xx = second_of(ax[5]), second_of(ax[6]), second_of(ax[7])
-        yy = second_of(ay[5]), second_of(ay[6]), second_of(ay[7])
-        zz = second_of(az[5]), second_of(az[6]), second_of(az[7])
-        J[0, i] = first_of(along_x(dy[6])) + first_of(along_x(dz[7])) - yy[0] - zz[0]
-        J[1, i] = first_of(along_x(dy[5])) - xx[1] - zz[1]
-        J[2, i] = first_of(along_x(dz[5])) - xx[2] - yy[2]
+        heat = 0.2 * norm + 0.1 * (jx * jx + jy * jy + jz * jz) * inverse
+        put(4, -advect(4) + heat / (1.5 * cs2))
+
         cross = (u[1] * bz - u[2] * by, u[2] * bx - u[0] * bz, u[0] * by - u[1] * bx)
         for n in range(3):
-            put(5 + n, cross[n] + 0.1 * (xx[n] + yy[n] + zz[n]))
+            put(5 + n, cross[n] + 0.1 * (axx[n] + ayy[n] + azz[n]))
         return c
 
     lax.fori_loop(0, 8, partial, 0)
-
-    for copy in edges:
-        copy.wait_recv()
-
-    def finish(i, c):
-        yz = [first_of(lambda s, j=j: GY[j, i + 3 + s]) for j in range(4)]
-        bx, by, bz = B[0, i], B[1, i], B[2, i]
-        jx, jy, jz = J[0, i], J[1, i] + yz[3], J[2, i] + yz[2]
-        inverse = jnp.exp(-F[0, i + 3])
-        cs2 = jnp.exp((5.0 / 3.0) * F[4, i + 3] + (2.0 / 3.0) * F[0, i + 3])
-        na_ref[1, i] = na_ref[1, i] + (jy * bz - jz * by) * inverse
-        na_ref[2, i] = na_ref[2, i] + (jz * bx - jx * bz) * inverse + (0.1 / 3.0) * yz[1]
-        na_ref[3, i] = na_ref[3, i] + (jx * by - jy * bx) * inverse + (0.1 / 3.0) * yz[0]
-        na_ref[4, i] = na_ref[4, i] + 0.1 * (jx * jx + jy * jy + jz * jz) * inverse / (1.5 * cs2)
-        return c
-
-    lax.fori_loop(0, 8, finish, 0)
 
     @pl.when(is_root)
     def _():
@@ -327,7 +326,7 @@
 
     top_ref[...] = down[...]
 
-    for copy in then_y + then_z + last_y + edges:
+    for copy in first + then_y + then_z + corners:
         copy.wait_send()
 
     @pl.when(jnp.logical_not(is_chief))
@@ -368,9 +367,8 @@
         scratch_shapes=[
             pltpu.VMEM((8, 14, 8, 256), F32),
             pltpu.VMEM((8, 8, 8, 256), F32),
-            pltpu.VMEM((8, 8, 8, 256), F32),
+            pltpu.VMEM((8, 14, 8, 256), F32),
             pltpu.VMEM((4, 14, 8, 256), F32),
-            pltpu.VMEM((3, 8, 8, 256), F32),
             pltpu.VMEM((3, 8, 8, 256), F32),
             pltpu.VMEM((8, 128), F32),
             pltpu.VMEM((1, 128), F32),
@@ -378,12 +376,12 @@
             pltpu.VMEM((PLANE, 1, 128), F32),
             pltpu.VMEM((1, 128), F32),
             pltpu.SemaphoreType.DMA((2,)),
-            pltpu.SemaphoreType.DMA((2, 6)),
-            pltpu.SemaphoreType.DMA((2, 6)),
+            pltpu.SemaphoreType.DMA((2, 4)),
+            pltpu.SemaphoreType.DMA((2, 4)),
             pltpu.SemaphoreType.DMA((2, 3)),
             pltpu.SemaphoreType.DMA((2, 3)),
-            pltpu.SemaphoreType.DMA((2,)),
-            pltpu.SemaphoreType.DMA((2,)),
+            pltpu.SemaphoreType.DMA((4, 2)),
+            pltpu.SemaphoreType.DMA((4, 2)),
             pltpu.SemaphoreType.DMA((4,)),
             pltpu.SemaphoreType.DMA((3,)),
         ],

time: 52 us -> 51.1 us (0.983)
  the two profiles are of different devices: /device:TPU:16 before, /device:TPU:6 now
where the time goes in v3:
time: 51.1 us; the launch traced here: 51 us
  Pallas kernels  50.3 us (98%)
  between operations  0.65 us (1%)
    pallas_call x1, Pallas kernels, local(): pl.pallas_call(substep, out_shape=(pltpu.VMEM(fields.shape, F32), pltpu.V...  49.3 us
    pallas_call x1, Pallas kernels, local(): pl.pallas_call(update, out_shape=(block, block, jax.ShapeDtypeStruct((1,)...  1.04 us

profile of v3, /device:TPU:6, one launch (start us, length us, event | category | flops | bytes accessed | tf_op | source)
XLA Modules:
  0.0 51.0 jit_solution(3202447022240147136)
XLA Ops:
  0.6 0.0 copy-start
  0.6 49.3 %shard_map.49 = (f32[8,8,8,256]{3,2,1,0:T(8,128)S(1)}, f32[1,128]{1,0:T(1,128)S(1)}) custom-call(f32[8,8,8,256]{3,2,1,0:T(8,128)} %f_ref.1, f32[8,8,8,256]{3,2,1,0:T(8,128)} %a_hbm.1), custom_call_target="tpu_custom_call" | custom-call | flops 13000000 | bytes 2000000 | tf_op jit(solution)/shard_map/pallas_call | solution.py:362
  49.9 0.0 copy-done
  49.9 1.0 %shard_map.50 = (f32[8,8,8,256]{3,2,1,0:T(8,128)}, f32[8,8,8,256]{3,2,1,0:T(8,128)}, f32[1]{0:T(128)}) custom-call(f32[8,8,8,256]{3,2,1,0:T(8,128)S(1)} %copy-done, f32[8,8,8,256]{3,2,1,0:T(8,128)S(1)} %get-tuple-element.5.na_ref, f32[1,128]{1,0:T(1,128)S(1)} %get-tuple-element.6.top_ref), custom_call_target="tpu_custom_call" | custom-call | flops 300000 | bytes 2500000 | tf_op jit(solution)/shard_map/pallas_call | solution.py:393
Async XLA Ops:
  0.6 49.3 %copy-start = (f32[8,8,8,256]{3,2,1,0:T(8,128)S(1)}, f32[8,8,8,256]{3,2,1,0:T(8,128)}, u32[]{:S(2)}) copy-start(f32[8,8,8,256]{3,2,1,0:T(8,128)} %f_ref.1) | copy-start | bytes 1572868

commit v4 on v3

--- a/solution.py
+++ b/solution.py
@@ -8,6 +8,7 @@
 MESH = pl.DeviceIdType.MESH
 F32 = jnp.float32
 MIXED = (2, 3, 6, 7)
+FIRST, SECOND = (0, 1), (2, 0)
 COLUMN = 8
 PLANE = 128
 
@@ -101,7 +102,9 @@
     level = gz // 8
     among = lax.rem(gy * 8 + gz + PLANE - 1, PLANE)
     is_chief = level == 0
-    is_root = jnp.logical_and(gy == 0, gz == 1)
+    is_first = jnp.logical_and(gy == 0, gz == 1)
+    is_second = jnp.logical_and(gy == 2, gz == 0)
+    is_root = jnp.logical_or(is_first, is_second)
 
     load_f = pltpu.make_async_copy(f_hbm, F.at[:, pl.ds(3, 8)], load_sem.at[0])
     load_a = pltpu.make_async_copy(a_hbm, A, load_sem.at[1])
@@ -122,7 +125,13 @@
         for i in range(1, COLUMN):
             pl.semaphore_signal(barrier, inc=1, device_id=(gy, gz + 8 * i), device_id_type=MESH)
 
-    pl.semaphore_wait(barrier, 5)
+    @pl.when(is_chief)
+    def _():
+        pl.semaphore_wait(barrier, 6)
+
+    @pl.when(jnp.logical_not(is_chief))
+    def _():
+        pl.semaphore_wait(barrier, 5)
 
     def remote(src, dst, send, recv, to):
         return pltpu.make_async_remote_copy(
@@ -199,8 +208,10 @@
     chief_id = (gy, lax.rem(gz, 8))
     to_chief = remote(own, ups.at[level], t_send.at[0], t_recv.at[0], chief_id)
     all_ups = remote(ups.at[pl.ds(1, COLUMN - 1)], ups.at[pl.ds(1, COLUMN - 1)], t_send.at[2], t_recv.at[0], chief_id)
-    to_root = remote(own, chiefs.at[among], t_send.at[1], t_recv.at[1], chief(0))
+    to_first = remote(own, chiefs.at[among], t_send.at[1], t_recv.at[1], FIRST)
+    to_second = remote(own, chiefs.at[among], t_send.at[4], t_recv.at[1], SECOND)
     all_chiefs = remote(chiefs.at[pl.ds(1, PLANE - 1)], chiefs.at[pl.ds(1, PLANE - 1)], t_send.at[3], t_recv.at[1], chief(0))
+    half_sends = remote(chiefs.at[pl.ds(1, PLANE // 2 - 1)], chiefs.at[pl.ds(1, PLANE // 2 - 1)], t_send.at[3], t_recv.at[1], chief(0))
     to_down = remote(down, down, t_send.at[2], t_recv.at[2], chief(0))
 
     @pl.when(jnp.logical_not(is_chief))
@@ -223,9 +234,13 @@
         all_ups.wait_recv()
         own[...] = jnp.maximum(own[...], jnp.max(ups[1:], axis=0))
 
-        @pl.when(jnp.logical_not(is_root))
+        @pl.when(jnp.logical_not(is_first))
         def _():
-            to_root.start()
+            to_first.start()
+
+        @pl.when(jnp.logical_not(is_second))
+        def _():
+            to_second.start()
 
     pl.when(gz == 0)(forward)
 
@@ -310,10 +325,18 @@
     @pl.when(is_root)
     def _():
         all_chiefs.wait_recv()
-        most = jnp.max(jnp.maximum(own[...], jnp.max(chiefs[1:], axis=0)))
+        chiefs[among] = own[...]
+        most = jnp.max(jnp.max(chiefs[...], axis=0))
         down[...] = jnp.full(down.shape, most, F32)
-        for i in NEAR_FIRST:
-            remote(down, down, t_send.at[3], t_recv.at[2], chief(i)).start()
+
+    for when, core in ((is_first, 1), (is_second, 0)):
+
+        @pl.when(when)
+        def _():
+            for i in [0, *NEAR_FIRST]:
+                to = chief(i)
+                if to[1] % 2 == core and to not in (FIRST, SECOND):
+                    remote(down, down, t_send.at[3], t_recv.at[2], to).start()
 
     @pl.when(jnp.logical_not(is_root))
     def _():
@@ -337,13 +360,17 @@
     def _():
         all_ups.wait_send()
 
-        @pl.when(jnp.logical_not(is_root))
+        @pl.when(jnp.logical_not(is_first))
         def _():
-            to_root.wait_send()
+            to_first.wait_send()
+
+        @pl.when(jnp.logical_not(is_second))
+        def _():
+            to_second.wait_send()
 
     @pl.when(is_root)
     def _():
-        all_chiefs.wait_send()
+        half_sends.wait_send()
 
 
 def update(f_ref, na_ref, top_ref, nf_ref, out_ref, dt_ref):
@@ -382,7 +409,7 @@
             pltpu.SemaphoreType.DMA((2, 3)),
             pltpu.SemaphoreType.DMA((4, 2)),
             pltpu.SemaphoreType.DMA((4, 2)),
-            pltpu.SemaphoreType.DMA((4,)),
+            pltpu.SemaphoreType.DMA((5,)),
             pltpu.SemaphoreType.DMA((3,)),
         ],
         compiler_params=pltpu.CompilerParams(

time: 51.1 us -> 54.1 us (1.059)
  the two profiles are of different devices: /device:TPU:6 before, /device:TPU:10 now
where the time goes in v4:
time: 54.1 us; the launch traced here: 53.9 us
  Pallas kernels  53.3 us (99%)
  between operations  0.65 us (1%)
    pallas_call x1, Pallas kernels, local(): pl.pallas_call(substep, out_shape=(pltpu.VMEM(fields.shape, F32), pltpu.V...  52.2 us

profile of v4, /device:TPU:10, one launch (start us, length us, event | category | flops | bytes accessed | tf_op | source)
XLA Modules:
  0.0 53.9 jit_solution(5587822232150705097)
XLA Ops:
  0.6 0.0 copy-start
  0.6 52.2 %shard_map.49 = (f32[8,8,8,256]{3,2,1,0:T(8,128)S(1)}, f32[1,128]{1,0:T(1,128)S(1)}) custom-call(f32[8,8,8,256]{3,2,1,0:T(8,128)} %f_ref.1, f32[8,8,8,256]{3,2,1,0:T(8,128)} %a_hbm.1), custom_call_target="tpu_custom_call" | custom-call | flops 13000000 | bytes 2000000 | tf_op jit(solution)/shard_map/pallas_call | solution.py:389
  52.9 0.0 copy-done
  52.9 1.0 %shard_map.50 = (f32[8,8,8,256]{3,2,1,0:T(8,128)}, f32[8,8,8,256]{3,2,1,0:T(8,128)}, f32[1]{0:T(128)}) custom-call(f32[8,8,8,256]{3,2,1,0:T(8,128)S(1)} %copy-done, f32[8,8,8,256]{3,2,1,0:T(8,128)S(1)} %get-tuple-element.5.na_ref, f32[1,128]{1,0:T(1,128)S(1)} %get-tuple-element.6.top_ref), custom_call_target="tpu_custom_call" | custom-call | flops 300000 | bytes 2500000 | tf_op jit(solution)/shard_map/pallas_call | solution.py:420
Async XLA Ops:
  0.6 52.3 %copy-start = (f32[8,8,8,256]{3,2,1,0:T(8,128)S(1)}, f32[8,8,8,256]{3,2,1,0:T(8,128)}, u32[]{:S(2)}) copy-start(f32[8,8,8,256]{3,2,1,0:T(8,128)} %f_ref.1) | copy-start | bytes 1572868
